TPU v7x, 256 devices: a whole 4x4x8 slice. The times are simulated.
256 devices in a mesh: mem: 64 (over x_hi, z, y), lat: 4 (over x_lo, core).
Axes of the slice: x: 4 (x_hi: 2, x_lo: 2; x = x_hi * 2 + x_lo), y: 4, z: 8, core: 2. Of those that a mesh axis runs over, the one named last changes fastest.
Arguments:
- gradient: bfloat16 [720, 5760], P('lat', 'mem'), may hold values from -6 to 6
- perturbations: bfloat16 [64, 720, 5760], P('mem', 'lat'), may hold values from -6 to 6
- lat_mix: float32 [720, 720], replicated, may hold values from -0.21875 to 0.21875
- zonal_weight: float32 [720], replicated, may hold values from 0.05 to 1
Outputs:
- increment: float32 [720, 5760], P('lat', 'mem')
All inputs are finite; a program needn't handle non-finite values.
Results may differ from a plain program's by a relative error of at most 0.0003.
Values may be sent and summed in bfloat16 or wider, within the bound.
A program may use at most 128 MiB of HBM per device.

v0:
```python
import math

import jax
import jax.numpy as jnp
import numpy as np
from jax import lax
from jax.experimental import pallas as pl
from jax.experimental.pallas import tpu as pltpu
from jax.sharding import PartitionSpec as P

MESH = pl.DeviceIdType.MESH
F32 = jnp.float32
BF16 = jnp.bfloat16
NLON = 1440
NWAVE = 720
MEMBERS = 64
ROWS = 180
HALF = 96
BAND = 192
UNIT = 90
WIDE = 360
LANES = 384
NZ, NY = 8, 4
LEFT = 384
TABLE = 1920


def wave_table():
    waves = np.arange(NWAVE)
    offsets = np.arange(TABLE) - LEFT
    gains = np.where(waves == 0, 1.0, 2.0) / NLON
    angles = (waves[:, None] * offsets[None, :] % NLON) * (2.0 * math.pi / NLON)
    return (gains[:, None] * np.cos(angles)).astype(np.float32)


class Copies:
    def __init__(self, send, recv):
        self.send, self.recv, self.count, self.made = send, recv, 0, []

    def start(self, src, dst, device):
        k = self.count
        self.count += 1
        copy = pltpu.make_async_remote_copy(
            src_ref=src,
            dst_ref=dst,
            send_sem=self.send.at[k],
            recv_sem=self.recv.at[k],
            device_id=device,
            device_id_type=MESH,
        )
        copy.start()
        self.made.append(copy)
        return copy


def gather_ring(copies, n, me, buf, half, plus, minus):
    k = n // 2
    up = copies.start(buf.at[me], buf.at[me], plus)
    down = copies.start(buf.at[me], buf.at[me], minus)
    for t in range(1, k):
        yield
        up_src = lax.rem(me - t + n, n)
        down_src = lax.rem(me + t, n)
        last = t == k - 1
        up.wait_recv()
        part = buf.at[up_src, pl.ds(0, half)] if last else buf.at[up_src]
        up = copies.start(part, part, plus)
        down.wait_recv()
        part = buf.at[down_src, pl.ds(half, half)] if last else buf.at[down_src]
        down = copies.start(part, part, minus)
    yield
    up.wait_recv()
    down.wait_recv()


def scatter_ring(copies, n, me, own, slots, half, plus, minus, finish):
    k = n // 2
    size = 2 * half
    up_slots, down_slots = slots.at[0], slots.at[1]
    far = lax.rem(me + k, n)
    for j in range(half):
        up_slots[k, j] = own(far, j)
        down_slots[k, half + j] = own(far, half + j)
    up = copies.start(
        up_slots.at[k, pl.ds(0, half)], up_slots.at[0, pl.ds(0, half)], plus
    )
    down = copies.start(
        down_slots.at[k, pl.ds(half, half)], down_slots.at[0, pl.ds(half, half)], minus
    )
    for t in range(1, k):
        yield
        up_dest = lax.rem(me + k - t, n)
        down_dest = lax.rem(me - k + t + n, n)
        up.wait_recv()
        for j in range(size):
            if t == 1 and j >= half:
                up_slots[t - 1, j] = own(up_dest, j)
            else:
                up_slots[t - 1, j] += own(up_dest, j)
        up = copies.start(up_slots.at[t - 1], up_slots.at[t], plus)
        down.wait_recv()
        for j in range(size):
            if t == 1 and j < half:
                down_slots[t - 1, j] = own(down_dest, j)
            else:
                down_slots[t - 1, j] += own(down_dest, j)
        down = copies.start(down_slots.at[t - 1], down_slots.at[t], minus)
    yield
    up.wait_recv()
    down.wait_recv()
    for j in range(size):
        finish(j, up_slots[k - 1, j] + down_slots[k - 1, j] + own(me, j))


def kernel(
    pert, grad, mix, weight, table, out,
    p_v, m_v, e_v, unit, yu, zu, gz, gy, pz, py, work, a32, ay, ag,
    mpad, mh, ml, ch, cl, rest, rest_y, s1, s2, s3, s4, t1, t2, ux, ur,
    local_sem, send_sem, recv_sem,
):
    mem, lat = lax.axis_index("mem"), lax.axis_index("lat")
    xh, z, y = mem // 32, (mem // 4) % NZ, mem % NY

    def member(xh_, z_, y_):
        return {"mem": xh_ * 32 + z_ * 4 + y_, "lat": lat}

    z_up, z_down = member(xh, (z + 1) % NZ, y), member(xh, (z + NZ - 1) % NZ, y)
    y_up, y_down = member(xh, z, (y + 1) % NY), member(xh, z, (y + NY - 1) % NY)
    x_far = member(1 - xh, z, y)
    chip_lat = (lat + 2) % 4
    core_lat = lat + 1 - 2 * (lat % 2)
    chip = {"mem": mem, "lat": chip_lat}
    core = {"mem": mem, "lat": core_lat}
    copies = Copies(send_sem, recv_sem)

    loads = [
        pltpu.make_async_copy(table, e_v, local_sem.at[0]),
        pltpu.make_async_copy(pert, p_v, local_sem.at[1]),
        pltpu.make_async_copy(mix, m_v, local_sem.at[2]),
    ]
    for load in loads:
        load.start()

    barrier = pltpu.get_barrier_semaphore()
    peers = (z_up, z_down, y_up, y_down, x_far, chip, core)
    for peer in peers:
        pl.semaphore_signal(barrier, inc=1, device_id=peer, device_id_type=MESH)
    unit[xh] = jnp.zeros((BAND, 128), BF16)
    unit[xh, 0:ROWS, 0:UNIT] = grad[...]
    pl.semaphore_wait(barrier, len(peers))

    x_copy = copies.start(unit.at[xh], unit.at[xh], x_far)

    tail = jnp.zeros((HALF, LANES - WIDE), BF16)
    for q in range(2 * NZ):
        pz[q, :, WIDE:] = tail
    for i in range(NY):
        a32[i, :, WIDE:] = jnp.zeros((BAND, LANES - WIDE), F32)
        rest_y[i, :, WIDE:] = jnp.zeros((HALF, LANES - WIDE), F32)
        for v in range(4):
            py[i, v, :, WIDE:] = tail
            py[i, v, 84:, :] = jnp.zeros((HALF - 84, LANES), BF16)
    for i in range(2):
        gz[z, i, :, WIDE:] = tail
    for v in range(4):
        gy[y, v, :, WIDE:] = tail

    def color_one():
        for i in range(2):
            yu[y, i] = unit[i, 0:HALF]
        yield from gather_ring(copies, NY, y, yu, 1, y_up, y_down)
        for i in range(2):
            for j in range(NY):
                gz[z, i, :, UNIT * j : UNIT * (j + 1)] = yu[j, i, :, 0:UNIT]
        yield from gather_ring(copies, NZ, z, gz, 1, z_up, z_down)

    def color_two():
        for i in range(2):
            zu[z, i] = unit[i, HALF:BAND]
        yield from gather_ring(copies, NZ, z, zu, 1, z_up, z_down)
        for i in range(2):
            for j in range(NZ):
                v, r = 2 * i + j // 4, j % 4
                gy[y, v, :, UNIT * r : UNIT * (r + 1)] = zu[j, i, :, 0:UNIT]
        yield from gather_ring(copies, NY, y, gy, 2, y_up, y_down)

    def stage_pz(v):
        if v == 0:
            loads[1].wait()
        for r in range(4):
            q = 4 * v + r
            pz[q, :, 0:WIDE] = p_v[0:HALF, WIDE * q : WIDE * (q + 1)]

    def stage_py(v):
        for i in range(NY):
            for r in range(4):
                c = WIDE * (4 * v + r) + UNIT * i
                py[i, v, 0:84, UNIT * r : UNIT * (r + 1)] = p_v[HALF:ROWS, c : c + UNIT]

    def stage_mix():
        loads[2].wait()
        odd = lat % 2
        first = pl.multiple_of(ROWS * lat - 4 * odd, 8)
        rows = m_v[pl.ds(first, ROWS + 4), :]
        rows = jnp.where(odd == 1, rows[4:], rows[:ROWS])
        mpad[...] = jnp.zeros((BAND, 4 * BAND), F32)
        for b in range(4):
            mpad[0:ROWS, BAND * b : BAND * b + ROWS] = rows[:, ROWS * b : ROWS * (b + 1)]
        full = mpad[...]
        high = full.astype(BF16)
        mh[...] = high
        ml[...] = (full - high.astype(F32)).astype(BF16)

    def stage_lags():
        loads[0].wait()
        row = jnp.broadcast_to(weight[...].reshape(1, NWAVE), (8, NWAVE))
        work[...] = jnp.dot(
            row, e_v[...], precision=lax.Precision.HIGHEST, preferred_element_type=F32
        )

    def stage_kernel(d):
        lags = jnp.concatenate(
            [
                work[0:1, LEFT + WIDE * d : LEFT + WIDE * d + LANES],
                work[0:1, WIDE * d : WIDE * d + LEFT],
            ],
            axis=1,
        )
        turned = pltpu.roll(
            jnp.broadcast_to(lags, (LANES, 2 * LANES)), 0, 1, stride=1, stride_axis=0
        )
        block = turned[:, :LANES]
        high = block.astype(BF16)
        low = (block - high.astype(F32)).astype(BF16)
        for r in range(4):
            s = (r + d) % 4
            ch[r, :, LANES * s : LANES * (s + 1)] = high
            cl[r, :, LANES * s : LANES * (s + 1)] = low

    stage_lags()
    x_copy.wait_recv()
    one, two = color_one(), color_two()
    next(one)
    next(two)
    stage_pz(0)
    next(one)
    next(two)
    stage_pz(1)
    next(one)
    next(two)
    stage_pz(2)
    next(two)
    stage_pz(3)
    next(one)
    next(two)
    stage_py(0)
    stage_py(1)
    stage_mix()
    next(one)
    stage_py(2)
    stage_py(3)
    stage_kernel(0)
    next(one)
    stage_kernel(1)
    next(two)
    stage_kernel(2)
    stage_kernel(3)
    next(one, None)
    for r in range(4):
        total = jnp.zeros((HALF, LANES), F32)
        for v in range(4):
            total += pz[4 * v + r].astype(F32) * gz[r + 4 * (v % 2), v // 2].astype(F32)
        a32[r, 0:HALF] = total
    next(two, None)
    for i in range(NY):
        total = jnp.zeros((HALF, LANES), F32)
        for v in range(4):
            total += py[i, v].astype(F32) * gy[i, v].astype(F32)
        ay[i] = total

    def band_rows(b):
        return pl.ds(pl.multiple_of(BAND * b, BAND), BAND)

    to_chip, to_core, passed = [], [], []
    for r in range(4):
        for i in range(NY):
            a32[r, HALF:BAND, UNIT * i : UNIT * (i + 1)] = ay[
                i, :, UNIT * r : UNIT * (r + 1)
            ]
        value = a32[r]
        high = value.astype(BF16)
        ag[r, band_rows(lat), 0:LANES] = high
        ag[r, band_rows(lat), LANES:] = (value - high.astype(F32)).astype(BF16)
        here = ag.at[r, band_rows(lat)]
        to_chip.append(copies.start(here, here, chip))
        to_core.append(copies.start(here, here, core))

    def localize(r):
        to_core[r].wait_recv()
        passed[r].wait_recv()
        both = jnp.dot(mh[...], ag[r], preferred_element_type=F32)
        low = jnp.dot(ml[...], ag[r, :, 0:LANES], preferred_element_type=F32)
        mixed = a32[r] + (both[:, :LANES] + (both[:, LANES:] + low))
        high = mixed.astype(BF16)
        low = (mixed - high.astype(F32)).astype(BF16)
        for s in range(4):
            cols = slice(LANES * s, LANES * (s + 1))
            term = jnp.dot(high, ch[r, :, cols], preferred_element_type=F32) + (
                jnp.dot(high, cl[r, :, cols], preferred_element_type=F32)
                + jnp.dot(low, ch[r, :, cols], preferred_element_type=F32)
            )
            if r == 0:
                rest[s] = term
            else:
                rest[s] += term

    for r in range(4):
        to_chip[r].wait_recv()
        there = ag.at[r, band_rows(chip_lat)]
        passed.append(copies.start(there, there, core))
        if r > 0:
            localize(r - 1)
    localize(3)

    def own_one(d, j):
        return pz[j * NZ + d].astype(F32) * rest[d % 4, 0:HALF]

    def own_two(d, j):
        return py[d, j].astype(F32) * rest_y[d]

    def store_one(j, value):
        for i in range(NY):
            t1[i, j, :, 0:UNIT] = value[:, UNIT * i : UNIT * (i + 1)]

    def store_two(j, value):
        for r in range(4):
            t2[r + 4 * (j % 2), j // 2, :, 0:UNIT] = value[:, UNIT * r : UNIT * (r + 1)]

    def last_one(j, value):
        ux[j, 0:HALF] = value

    def last_two(j, value):
        ux[j, HALF:BAND] = value

    def sum_one():
        yield from scatter_ring(copies, NZ, z, own_one, s1, 1, z_up, z_down, store_one)
        yield from scatter_ring(
            copies, NY, y, lambda d, j: t1[d, j], s3, 1, y_up, y_down, last_one
        )

    def sum_two():
        for i in range(NY):
            for r in range(4):
                rest_y[i, :, UNIT * r : UNIT * (r + 1)] = rest[
                    r, HALF:BAND, UNIT * i : UNIT * (i + 1)
                ]
        yield from scatter_ring(copies, NY, y, own_two, s2, 2, y_up, y_down, store_two)
        yield from scatter_ring(
            copies, NZ, z, lambda d, j: t2[d, j], s4, 1, z_up, z_down, last_two
        )

    one, two = sum_one(), sum_two()
    for chain in (one, two, one, two, one, one, two, two, one, two, two, one, one, two):
        next(chain, None)
    x_copy = copies.start(ux.at[1 - xh], ur, x_far)
    x_copy.wait_recv()
    total = (ux[xh] + ur[...]) * (1.0 / math.sqrt(MEMBERS - 1))
    out[...] = total[0:ROWS, 0:UNIT]
    for copy in copies.made:
        copy.wait_send()


def local(gradient, perturbations, lat_mix, zonal_weight):
    vmem = pl.BlockSpec(memory_space=pltpu.VMEM)
    hbm = pl.BlockSpec(memory_space=pl.ANY)
    return pl.pallas_call(
        kernel,
        out_shape=jax.ShapeDtypeStruct((ROWS, UNIT), F32),
        in_specs=[hbm, vmem, hbm, vmem, hbm],
        out_specs=vmem,
        scratch_shapes=[
            pltpu.VMEM((ROWS, 4 * NLON), BF16),
            pltpu.VMEM((720, 720), F32),
            pltpu.VMEM((NWAVE, TABLE), F32),
            pltpu.VMEM((2, BAND, 128), BF16),
            pltpu.VMEM((NY, 2, HALF, 128), BF16),
            pltpu.VMEM((NZ, 2, HALF, 128), BF16),
            pltpu.VMEM((NZ, 2, HALF, LANES), BF16),
            pltpu.VMEM((NY, 4, HALF, LANES), BF16),
            pltpu.VMEM((2 * NZ, HALF, LANES), BF16),
            pltpu.VMEM((NY, 4, HALF, LANES), BF16),
            pltpu.VMEM((8, TABLE), F32),
            pltpu.VMEM((4, BAND, LANES), F32),
            pltpu.VMEM((NY, HALF, LANES), F32),
            pltpu.VMEM((4, 4 * BAND, 2 * LANES), BF16),
            pltpu.VMEM((BAND, 4 * BAND), F32),
            pltpu.VMEM((BAND, 4 * BAND), BF16),
            pltpu.VMEM((BAND, 4 * BAND), BF16),
            pltpu.VMEM((4, LANES, 4 * LANES), BF16),
            pltpu.VMEM((4, LANES, 4 * LANES), BF16),
            pltpu.VMEM((4, BAND, LANES), F32),
            pltpu.VMEM((NY, HALF, LANES), F32),
            pltpu.VMEM((2, NZ // 2 + 1, 2, HALF, LANES), F32),
            pltpu.VMEM((2, NY // 2 + 1, 4, HALF, LANES), F32),
            pltpu.VMEM((2, NY // 2 + 1, 2, HALF, 128), F32),
            pltpu.VMEM((2, NZ // 2 + 1, 2, HALF, 128), F32),
            pltpu.VMEM((NY, 2, HALF, 128), F32),
            pltpu.VMEM((NZ, 2, HALF, 128), F32),
            pltpu.VMEM((2, BAND, 128), F32),
            pltpu.VMEM((BAND, 128), F32),
            pltpu.SemaphoreType.DMA((3,)),
            pltpu.SemaphoreType.DMA((64,)),
            pltpu.SemaphoreType.DMA((64,)),
        ],
        compiler_params=pltpu.CompilerParams(
            collective_id=0, has_side_effects=True, vmem_limit_bytes=56 * 2**20
        ),
    )(
        perturbations.reshape(ROWS, 4 * NLON),
        gradient,
        lat_mix,
        zonal_weight,
        jnp.asarray(wave_table()),
    )


def solution(mesh):
    return jax.shard_map(
        local,
        mesh=mesh,
        in_specs=(P("lat", "mem"), P("mem", "lat", None), P(), P()),
        out_specs=P("lat", "mem"),
        check_vma=False,
    )
```

profile of v0, /device:TPU:8, one launch (start us, length us, event | category | flops | bytes accessed | tf_op | source)
XLA Modules:
  0.0 117.4 jit_solution(4967210139404824305)
XLA Ops:
  0.0 115.9 %shard_map.55 = f32[180,90]{1,0:T(8,128)} custom-call(bf16[180,5760]{1,0:T(8,128)(2,1)} %bitcast.1, bf16[180,90]{1,0:T(8,128)(2,1)} %grad.1, f32[720,720]{1,0:T(8,128)} %mix.1, f32[720]{0:T(1024)} %weight.1, f32[720,1920]{1,0:T(8,128)} %constant.2.clone.table), custom_call_target="tpu_custom_call" | custom-call | tf_op jit(solution)/shard_map/pallas_call | solution.py:376
  115.9 1.5 %copy.7 = f32[180,90]{1,0:T(8,128)} copy(f32[180,90]{1,0:T(8,128)} %shard_map.55) | data formatting | bytes 129600
where the time goes:
time: 118 us; the launch traced here: 117 us
  Pallas kernels  116 us (98%)
  local copies, waits for them, and re-layouts  1.54 us (1%)
    pallas_call x1, Pallas kernels, local(): pl.pallas_call(kernel, out_shape=jax.ShapeDtypeStruct((ROWS, UNIT), F32),...  116 us

commit v1 on v0

v1 whole, which is shorter than its diff:
```python
import math

import jax
import jax.numpy as jnp
import numpy as np
from jax import lax
from jax.experimental import pallas as pl
from jax.experimental.pallas import tpu as pltpu
from jax.sharding import PartitionSpec as P

MESH = pl.DeviceIdType.MESH
F32 = jnp.float32
BF16 = jnp.bfloat16
NLON = 1440
NWAVE = 720
MEMBERS = 64
ROWS = 180
BAND = 192
ONE = 112
TWO = BAND - ONE
REAL = ROWS - ONE
FLOAT = (REAL + 7) // 8 * 8
UNIT = 90
WIDE = 360
LANES = 384
NZ, NY = 8, 4
LEFT = 384
TABLE = 1920


def wave_table():
    waves = np.arange(NWAVE)
    offsets = np.arange(TABLE) - LEFT
    gains = np.where(waves == 0, 1.0, 2.0) / NLON
    angles = (waves[:, None] * offsets[None, :] % NLON) * (2.0 * math.pi / NLON)
    return (gains[:, None] * np.cos(angles)).astype(np.float32)


class Copies:
    def __init__(self, send, recv):
        self.send, self.recv, self.count, self.made = send, recv, 0, []

    def start(self, src, dst, device):
        k = self.count
        self.count += 1
        copy = pltpu.make_async_remote_copy(
            src_ref=src,
            dst_ref=dst,
            send_sem=self.send.at[k],
            recv_sem=self.recv.at[k],
            device_id=device,
            device_id_type=MESH,
        )
        copy.start()
        self.made.append(copy)
        return copy


def gather_ring(copies, n, me, buf, half, plus, minus):
    k = n // 2
    parts = (pl.ds(0, half), pl.ds(half, half))
    up, down = {}, {}
    for j in (0, 1):
        mine = buf.at[me, parts[j]]
        up[j] = copies.start(mine, mine, plus)
        down[1 - j] = copies.start(
            buf.at[me, parts[1 - j]], buf.at[me, parts[1 - j]], minus
        )
    for t in range(1, k):
        yield t
        for j in (0, 1):
            i = 1 - j
            up[j].wait_recv()
            if t < k - 1 or j == 0:
                there = buf.at[lax.rem(me - t + n, n), parts[j]]
                up[j] = copies.start(there, there, plus)
            down[i].wait_recv()
            if t < k - 1 or i == 1:
                there = buf.at[lax.rem(me + t, n), parts[i]]
                down[i] = copies.start(there, there, minus)
    yield k
    up[0].wait_recv()
    down[1].wait_recv()


def scatter_ring(copies, n, me, own, first, slots, half, plus, minus, finish):
    k = n // 2
    low, high = range(half), range(half, 2 * half)
    up, down = {}, {}

    def begin(way, dest, j, t, device, made):
        first[way, j] = own(dest, j)
        made[j] = copies.start(first.at[way, j], slots.at[way, t, j], device)

    def forward(way, dest, j, t, device, made):
        made[j].wait_recv()
        slots[way, t - 1, j] += own(dest, j)
        made[j] = copies.start(slots.at[way, t - 1, j], slots.at[way, t, j], device)

    for a, b in zip(low, high):
        begin(0, lax.rem(me + k, n), a, 0, plus, up)
        begin(1, lax.rem(me + k, n), b, 0, minus, down)
    for a, b in zip(low, high):
        begin(0, lax.rem(me + k - 1, n), b, 1, plus, up)
        begin(1, lax.rem(me - k + 1 + n, n), a, 1, minus, down)
    for t in range(1, k):
        yield
        up_dest = lax.rem(me + k - t, n)
        down_dest = lax.rem(me - k + t + n, n)
        if t > 1:
            for a, b in zip(low, high):
                forward(0, up_dest, b, t, plus, up)
                forward(1, down_dest, a, t, minus, down)
        for a, b in zip(low, high):
            forward(0, up_dest, a, t, plus, up)
            forward(1, down_dest, b, t, minus, down)
    yield
    for j in (*high, *low):
        up[j].wait_recv()
        down[j].wait_recv()
        finish(j, slots[0, k - 1, j] + slots[1, k - 1, j] + own(me, j))


def kernel(
    pert, grad, mix, weight, table, out,
    p_v, m_v, e_v, yu, zu, gz, gy, pz, py, work, own_two, ag_one, ag_two,
    mpad, mh_one, ml_one, mh_two, ml_two, ch, cl, local, rest, rest_y,
    f1, s1, f2, s2, s4, t1, t2, p1, p2,
    local_sem, send_sem, recv_sem,
):
    mem, lat = lax.axis_index("mem"), lax.axis_index("lat")
    xh, z, y = mem // 32, (mem // 4) % NZ, mem % NY

    def member(dx, dz, dy):
        there = (
            lax.rem(xh + dx, 2) * 32 + lax.rem(z + dz, NZ) * 4 + lax.rem(y + dy, NY)
        )
        return {"mem": there, "lat": lat}

    z_up, z_down = member(0, 1, 0), member(0, NZ - 1, 0)
    y_up, y_down = member(0, 0, 1), member(0, 0, NY - 1)
    x_far, x_up, x_down = member(1, 0, 0), member(1, 1, 0), member(1, NZ - 1, 0)
    chip_lat = lax.rem(lat + 2, 4)
    chip = {"mem": mem, "lat": chip_lat}
    core = {"mem": mem, "lat": lat + 1 - 2 * lax.rem(lat, 2)}
    plane = [(dx, dy) for dx in range(2) for dy in range(NY) if (dx, dy) != (0, 0)]
    copies = Copies(send_sem, recv_sem)

    loads = [
        pltpu.make_async_copy(pert, p_v, local_sem.at[0]),
        pltpu.make_async_copy(table, e_v, local_sem.at[1]),
        pltpu.make_async_copy(mix, m_v, local_sem.at[2]),
    ]
    for load in loads:
        load.start()

    barrier = pltpu.get_barrier_semaphore()
    peers = [member(dx, 0, dy) for dx, dy in plane]
    peers += [z_up, z_down, x_up, x_down, chip, core]
    for peer in peers:
        pl.semaphore_signal(barrier, inc=1, device_id=peer, device_id_type=MESH)
    yu[xh, y] = jnp.zeros((ONE, 128), BF16)
    yu[xh, y, :, 0:UNIT] = grad[0:ONE]
    zu[z, xh] = jnp.zeros((TWO, 128), BF16)
    zu[z, xh, 0:REAL, 0:UNIT] = grad[ONE:ROWS]
    pl.semaphore_wait(barrier, len(peers))

    pieces = []

    def band_rows(b, rows):
        return pl.ds(pl.multiple_of(b * rows, 16), rows)

    def send_piece(ag, index, rows, value):
        high = value.astype(BF16)
        ag[index, band_rows(lat, rows), 0:LANES] = high
        ag[index, band_rows(lat, rows), LANES:] = (value - high.astype(F32)).astype(BF16)
        here = ag.at[index, band_rows(lat, rows)]
        there = ag.at[index, band_rows(chip_lat, rows)]
        pieces.append(
            {
                "index": index,
                "one": rows == ONE,
                "there": there,
                "chip": copies.start(here, here, chip),
                "core": copies.start(here, here, core),
            }
        )

    def pass_piece(k):
        piece = pieces[k]
        piece["chip"].wait_recv()
        piece["passed"] = copies.start(piece["there"], piece["there"], core)

    def mixed(high, low, ag, index):
        both = jnp.dot(high[...], ag[index], preferred_element_type=F32)
        return both[:, :LANES] + (
            both[:, LANES:]
            + jnp.dot(low[...], ag[index, :, 0:LANES], preferred_element_type=F32)
        )

    def mix_piece(k):
        piece = pieces[k]
        piece["core"].wait_recv()
        piece["passed"].wait_recv()
        index = piece["index"]
        if piece["one"]:
            local[index] += mixed(mh_one, ml_one, ag_one, index)
        else:
            work_y[...] = mixed(mh_two, ml_two, ag_two, index)
            for i in range(NY):

                @pl.when(index == i)
                def _():
                    for r in range(4):
                        local[r, :, UNIT * i : UNIT * (i + 1)] += work_y[
                            :, UNIT * r : UNIT * (r + 1)
                        ]

    work_y = own_two

    def piece_one(r):
        total = jnp.zeros((ONE, LANES), F32)
        for v in range(4):
            total += pz[4 * v + r].astype(F32) * gz[r + 4 * (v % 2), v // 2].astype(F32)
        send_piece(ag_one, r, ONE, total)
        local[r, 0:ONE] += total

    def piece_two(i):
        total = jnp.zeros((TWO, LANES), F32)
        for v in range(4):
            total += py[i, v].astype(F32) * gy[i, v].astype(F32)
        send_piece(ag_two, i, TWO, total)
        own_two[0:TWO] = total
        for i_ in range(NY):

            @pl.when(i == i_)
            def _():
                for r in range(4):
                    local[r, ONE:BAND, UNIT * i_ : UNIT * (i_ + 1)] += own_two[
                        0:TWO, UNIT * r : UNIT * (r + 1)
                    ]

    def color_one():
        mine = yu.at[xh, y]
        arriving = [copies.start(mine, mine, member(dx, 0, dy)) for dx, dy in plane]
        yield
        for copy in arriving:
            copy.wait_recv()
        for i in range(2):
            for j in range(NY):
                gz[z, i, :, UNIT * j : UNIT * (j + 1)] = yu[i, j, :, 0:UNIT]
        for t in gather_ring(copies, NZ, z, gz, 1, z_up, z_down):
            if t == 3:
                piece_one(lax.rem(z + 2, 4))
            if t == 4:
                piece_one(lax.rem(z + 1, 4))
                piece_one(lax.rem(z + 3, 4))
            yield
        piece_one(lax.rem(z, 4))

    def color_two():
        mine = zu.at[z, xh]
        up = [copies.start(mine, mine, z_up)]
        down = [copies.start(mine, mine, z_down)]
        far = copies.start(mine, mine, x_far)
        up.append(copies.start(mine, mine, x_up))
        down.append(copies.start(mine, mine, x_down))
        for t in range(1, NZ // 2):
            yield
            for copy in up:
                copy.wait_recv()
            there = zu.at[lax.rem(z + NZ - t, NZ)]
            if t == NZ // 2 - 1:
                there = zu.at[lax.rem(z + NZ - t, NZ), pl.ds(0, 1)]
            up = [copies.start(there, there, z_up)]
            for copy in down:
                copy.wait_recv()
            there = zu.at[lax.rem(z + t, NZ)]
            if t == NZ // 2 - 1:
                there = zu.at[lax.rem(z + t, NZ), pl.ds(1, 1)]
            down = [copies.start(there, there, z_down)]
        yield
        for copy in (far, *up, *down):
            copy.wait_recv()
        for i in range(2):
            for j in range(NZ):
                v, r = 2 * i + j // 4, j % 4
                gy[y, v, :, UNIT * r : UNIT * (r + 1)] = zu[j, i, :, 0:UNIT]
        for t in gather_ring(copies, NY, y, gy, 2, y_up, y_down):
            if t == 1:
                piece_two(y)
            if t == 2:
                piece_two(lax.rem(y + 1, NY))
                piece_two(lax.rem(y + 3, NY))
            yield
        piece_two(lax.rem(y + 2, NY))

    def stage_zeros():
        for q in range(2 * NZ):
            pz[q, :, WIDE:] = jnp.zeros((ONE, LANES - WIDE), BF16)
        for i in range(NY):
            local[i] = jnp.zeros((BAND, LANES), F32)
            rest_y[i, :, WIDE:] = jnp.zeros((FLOAT, LANES - WIDE), F32)
            for v in range(4):
                py[i, v, :, WIDE:] = jnp.zeros((TWO, LANES - WIDE), BF16)
                py[i, v, REAL:, :] = jnp.zeros((TWO - REAL, LANES), BF16)
        for i in range(2):
            gz[z, i, :, WIDE:] = jnp.zeros((ONE, LANES - WIDE), BF16)
        for v in range(4):
            gy[y, v, :, WIDE:] = jnp.zeros((TWO, LANES - WIDE), BF16)

    def stage_pz(v):
        for r in range(4):
            q = 4 * v + r
            pz[q, :, 0:WIDE] = p_v[0:ONE, WIDE * q : WIDE * (q + 1)]

    def stage_py(v):
        for i in range(NY):
            for r in range(4):
                c = WIDE * (4 * v + r) + UNIT * i
                py[i, v, 0:REAL, UNIT * r : UNIT * (r + 1)] = p_v[ONE:ROWS, c : c + UNIT]

    def stage_mix():
        loads[2].wait()
        odd = lax.rem(lat, 2)
        first = pl.multiple_of(ROWS * lat - 4 * odd, 8)
        rows = m_v[pl.ds(first, ROWS + 4), :]
        rows = jnp.where(odd == 1, rows[4:], rows[:ROWS])
        mpad[...] = jnp.zeros((BAND, 4 * BAND), F32)
        for b in range(4):
            c = ROWS * b
            mpad[0:ROWS, ONE * b : ONE * (b + 1)] = rows[:, c : c + ONE]
            d = 4 * ONE + TWO * b
            mpad[0:ROWS, d : d + REAL] = rows[:, c + ONE : c + ROWS]
        for high, low, full in (
            (mh_one, ml_one, mpad[:, 0 : 4 * ONE]),
            (mh_two, ml_two, mpad[:, 4 * ONE :]),
        ):
            rounded = full.astype(BF16)
            high[...] = rounded
            low[...] = (full - rounded.astype(F32)).astype(BF16)

    def stage_lags():
        loads[1].wait()
        row = jnp.broadcast_to(weight[...].reshape(1, NWAVE), (8, NWAVE))
        work[...] = jnp.dot(
            row, e_v[...], precision=lax.Precision.HIGHEST, preferred_element_type=F32
        )

    def stage_kernel(d):
        lags = jnp.concatenate(
            [
                work[0:1, LEFT + WIDE * d : LEFT + WIDE * d + LANES],
                work[0:1, WIDE * d : WIDE * d + LEFT],
            ],
            axis=1,
        )
        turned = pltpu.roll(
            jnp.broadcast_to(lags, (LANES, 2 * LANES)), 0, 1, stride=1, stride_axis=0
        )
        block = turned[:, :LANES]
        high = block.astype(BF16)
        low = (block - high.astype(F32)).astype(BF16)
        for r in range(4):
            s = (r + d) % 4
            place = (
                slice(LANES * r, LANES * (r + 1)),
                slice(LANES * s, LANES * (s + 1)),
            )
            ch[place] = high
            cl[place] = low

    one, two = color_one(), color_two()
    next(one)
    next(two)
    stage_zeros()
    loads[0].wait()
    stage_pz(0)
    next(one)
    stage_pz(1)
    next(two)
    stage_pz(2)
    stage_pz(3)
    next(one)
    next(two)
    stage_py(0)
    stage_py(1)
    next(two)
    next(one)
    stage_py(2)
    stage_py(3)
    next(two)
    next(one)
    stage_mix()
    stage_lags()
    pass_piece(0)
    next(one, None)
    stage_kernel(0)
    pass_piece(1)
    stage_kernel(1)
    pass_piece(2)
    next(two)
    stage_kernel(2)
    stage_kernel(3)
    next(two, None)
    pass_piece(3)
    for k in range(4):
        mix_piece(k)
        pass_piece(4 + k)
    for k in range(4, 8):
        mix_piece(k)

    def restore(rows):
        value = jnp.concatenate([local[r, rows] for r in range(4)], axis=1)
        high = value.astype(BF16)
        low = (value - high.astype(F32)).astype(BF16)
        for s in range(4):
            cols = slice(LANES * s, LANES * (s + 1))
            rest[s, rows] = jnp.dot(high, ch[:, cols], preferred_element_type=F32) + (
                jnp.dot(high, cl[:, cols], preferred_element_type=F32)
                + jnp.dot(low, ch[:, cols], preferred_element_type=F32)
            )

    def term_one(d, j):
        return pz[j * NZ + d].astype(F32) * rest[lax.rem(d, 4), 0:ONE]

    def term_two(d, j):
        return py[d, j, 0:FLOAT].astype(F32) * rest_y[d]

    def store_one(j, value):
        for i in range(NY):
            t1[j, i, :, 0:UNIT] = value[:, UNIT * i : UNIT * (i + 1)]

    def store_two(j, value):
        for r in range(4):
            t2[r + 4 * (j % 2), j // 2, :, 0:UNIT] = value[:, UNIT * r : UNIT * (r + 1)]

    scale = 1.0 / math.sqrt(MEMBERS - 1)

    def sum_one():
        restore(slice(0, ONE))
        yield from scatter_ring(
            copies, NZ, z, term_one, f1, s1, 1, z_up, z_down, store_one
        )
        arriving = []
        for k, (dx, dy) in enumerate(plane):
            part = t1.at[lax.rem(xh + dx, 2), lax.rem(y + dy, NY)]
            arriving.append(copies.start(part, p1.at[k], member(dx, 0, dy)))
        yield
        total = t1[xh, y]
        for k, copy in enumerate(arriving):
            copy.wait_recv()
            total += p1[k]
        out[0:ONE, :] = (total * scale)[:, 0:UNIT]

    def sum_two():
        restore(slice(ONE, BAND))
        for i in range(NY):
            for r in range(4):
                rest_y[i, :, UNIT * r : UNIT * (r + 1)] = rest[
                    r, ONE : ONE + FLOAT, UNIT * i : UNIT * (i + 1)
                ]
        yield from scatter_ring(
            copies, NY, y, term_two, f2, s2, 2, y_up, y_down, store_two
        )
        last = NZ // 2 - 1
        far = lax.rem(z + NZ // 2, NZ)
        cross = copies.start(t2.at[z, 1 - xh], p2.at[4], x_far)
        up = copies.start(t2.at[far, pl.ds(0, 1)], s4.at[0, 0, pl.ds(0, 1)], z_up)
        down = copies.start(t2.at[far, pl.ds(1, 1)], s4.at[1, 0, pl.ds(1, 1)], z_down)
        for t in range(1, NZ // 2):
            yield
            made = []
            for way, copy, dest, near, aside in (
                (0, up, lax.rem(z + NZ // 2 - t, NZ), z_up, x_up),
                (1, down, lax.rem(z + NZ // 2 + t, NZ), z_down, x_down),
            ):
                copy.wait_recv()
                for j in range(2):
                    if t == 1 and j != way:
                        s4[way, t - 1, j] = t2[dest, j]
                    else:
                        s4[way, t - 1, j] += t2[dest, j]
                if t < last:
                    made.append(copies.start(s4.at[way, t - 1], s4.at[way, t], near))
                else:
                    made.append(
                        (
                            copies.start(s4.at[way, t - 1, xh], p2.at[2 * way], near),
                            copies.start(
                                s4.at[way, t - 1, 1 - xh], p2.at[2 * way + 1], aside
                            ),
                        )
                    )
            up, down = made
        yield
        for copy in (cross, *up, *down):
            copy.wait_recv()
        total = t2[z, xh]
        for k in range(5):
            total += p2[k]
        out[ONE:ROWS, :] = (total * scale)[0:REAL, 0:UNIT]

    one, two = sum_one(), sum_two()
    for chain in (one, two, one, two, one, two, one, two, two, one, two, two, one):
        next(chain, None)
    for copy in copies.made:
        copy.wait_send()


def local(gradient, perturbations, lat_mix, zonal_weight):
    vmem = pl.BlockSpec(memory_space=pltpu.VMEM)
    hbm = pl.BlockSpec(memory_space=pl.ANY)
    return pl.pallas_call(
        kernel,
        out_shape=jax.ShapeDtypeStruct((ROWS, UNIT), F32),
        in_specs=[hbm, vmem, hbm, vmem, hbm],
        out_specs=vmem,
        scratch_shapes=[
            pltpu.VMEM((ROWS, 4 * NLON), BF16),
            pltpu.VMEM((720, 720), F32),
            pltpu.VMEM((NWAVE, TABLE), F32),
            pltpu.VMEM((2, NY, ONE, 128), BF16),
            pltpu.VMEM((NZ, 2, TWO, 128), BF16),
            pltpu.VMEM((NZ, 2, ONE, LANES), BF16),
            pltpu.VMEM((NY, 4, TWO, LANES), BF16),
            pltpu.VMEM((2 * NZ, ONE, LANES), BF16),
            pltpu.VMEM((NY, 4, TWO, LANES), BF16),
            pltpu.VMEM((8, TABLE), F32),
            pltpu.VMEM((BAND, LANES), F32),
            pltpu.VMEM((4, 4 * ONE, 2 * LANES), BF16),
            pltpu.VMEM((4, 4 * TWO, 2 * LANES), BF16),
            pltpu.VMEM((BAND, 4 * BAND), F32),
            pltpu.VMEM((BAND, 4 * ONE), BF16),
            pltpu.VMEM((BAND, 4 * ONE), BF16),
            pltpu.VMEM((BAND, 4 * TWO), BF16),
            pltpu.VMEM((BAND, 4 * TWO), BF16),
            pltpu.VMEM((4 * LANES, 4 * LANES), BF16),
            pltpu.VMEM((4 * LANES, 4 * LANES), BF16),
            pltpu.VMEM((4, BAND, LANES), F32),
            pltpu.VMEM((4, BAND, LANES), F32),
            pltpu.VMEM((NY, FLOAT, LANES), F32),
            pltpu.VMEM((2, 2, ONE, LANES), F32),
            pltpu.VMEM((2, NZ // 2, 2, ONE, LANES), F32),
            pltpu.VMEM((2, 4, FLOAT, LANES), F32),
            pltpu.VMEM((2, NY // 2, 4, FLOAT, LANES), F32),
            pltpu.VMEM((2, NZ // 2 - 1, 2, FLOAT, 128), F32),
            pltpu.VMEM((2, NY, ONE, 128), F32),
            pltpu.VMEM((NZ, 2, FLOAT, 128), F32),
            pltpu.VMEM((7, ONE, 128), F32),
            pltpu.VMEM((5, FLOAT, 128), F32),
            pltpu.SemaphoreType.DMA((3,)),
            pltpu.SemaphoreType.DMA((128,)),
            pltpu.SemaphoreType.DMA((128,)),
        ],
        compiler_params=pltpu.CompilerParams(
            collective_id=0, has_side_effects=True, vmem_limit_bytes=56 * 2**20
        ),
    )(
        perturbations.reshape(ROWS, 4 * NLON),
        gradient,
        lat_mix,
        zonal_weight,
        jnp.asarray(wave_table()),
    )


def solution(mesh):
    return jax.shard_map(
        local,
        mesh=mesh,
        in_specs=(P("lat", "mem"), P("mem", "lat", None), P(), P()),
        out_specs=P("lat", "mem"),
        check_vma=False,
    )
```

time: 118 us -> 102 us (0.86)
  Pallas kernels: 116 us -> 100 us
    pallas_call x1, Pallas kernels: 116 us -> 100 us  [local(): pl.pallas_call(kernel, out_shape=jax.ShapeDtypeStruct((ROWS, UNIT), F32),...]
where the time goes in v1:
time: 102 us
  Pallas kernels  100 us (98%)
  local copies, waits for them, and re-layouts  1.54 us (2%)
    pallas_call x1, Pallas kernels, local(): pl.pallas_call(kernel, out_shape=jax.ShapeDtypeStruct((ROWS, UNIT), F32),...  100 us

profile of v1, /device:TPU:8, one launch (start us, length us, event | category | flops | bytes accessed | tf_op | source)
XLA Modules:
  0.0 101.9 jit_solution(3991381261547342383)
XLA Ops:
  0.0 100.3 %shard_map.55 = f32[180,90]{1,0:T(8,128)} custom-call(bf16[180,5760]{1,0:T(8,128)(2,1)} %bitcast.1, bf16[180,90]{1,0:T(8,128)(2,1)} %grad.1, f32[720,720]{1,0:T(8,128)} %mix.1, f32[720]{0:T(1024)} %weight.1, f32[720,1920]{1,0:T(8,128)} %constant.2.clone.table), custom_call_target="tpu_custom_call" | custom-call | tf_op jit(solution)/shard_map/pallas_call | solution.py:514
  100.3 1.5 %copy.7 = f32[180,90]{1,0:T(8,128)} copy(f32[180,90]{1,0:T(8,128)} %shard_map.55) | data formatting | bytes 129600

commit v2 on v1

--- a/solution.py
+++ b/solution.py
@@ -17,6 +17,7 @@
 ROWS = 180
 BAND = 192
 ONE = 112
+CUT = 64
 TWO = BAND - ONE
 REAL = ROWS - ONE
 FLOAT = (REAL + 7) // 8 * 8
@@ -56,31 +57,27 @@
         return copy
 
 
-def gather_ring(copies, n, me, buf, half, plus, minus):
+def gather_ring(copies, n, me, pick, parts, plus, minus):
     k = n // 2
-    parts = (pl.ds(0, half), pl.ds(half, half))
+    early, late = range(parts // 2), range(parts // 2, parts)
     up, down = {}, {}
-    for j in (0, 1):
-        mine = buf.at[me, parts[j]]
-        up[j] = copies.start(mine, mine, plus)
-        down[1 - j] = copies.start(
-            buf.at[me, parts[1 - j]], buf.at[me, parts[1 - j]], minus
-        )
+    for i, j in zip((*early, *late), (*late, *early)):
+        up[i] = copies.start(pick(me, i), pick(me, i), plus)
+        down[j] = copies.start(pick(me, j), pick(me, j), minus)
     for t in range(1, k):
         yield t
-        for j in (0, 1):
-            i = 1 - j
-            up[j].wait_recv()
-            if t < k - 1 or j == 0:
-                there = buf.at[lax.rem(me - t + n, n), parts[j]]
-                up[j] = copies.start(there, there, plus)
-            down[i].wait_recv()
-            if t < k - 1 or i == 1:
-                there = buf.at[lax.rem(me + t, n), parts[i]]
-                down[i] = copies.start(there, there, minus)
+        up_src, down_src = lax.rem(me - t + n, n), lax.rem(me + t, n)
+        for i, j in zip((*early, *late), (*late, *early)):
+            up[i].wait_recv()
+            if t < k - 1 or i in early:
+                up[i] = copies.start(pick(up_src, i), pick(up_src, i), plus)
+            down[j].wait_recv()
+            if t < k - 1 or j in late:
+                down[j] = copies.start(pick(down_src, j), pick(down_src, j), minus)
     yield k
-    up[0].wait_recv()
-    down[1].wait_recv()
+    for i, j in zip(early, late):
+        up[i].wait_recv()
+        down[j].wait_recv()
 
 
 def scatter_ring(copies, n, me, own, first, slots, half, plus, minus, finish):
@@ -125,7 +122,7 @@
     pert, grad, mix, weight, table, out,
     p_v, m_v, e_v, yu, zu, gz, gy, pz, py, work, own_two, ag_one, ag_two,
     mpad, mh_one, ml_one, mh_two, ml_two, ch, cl, local, rest, rest_y,
-    f1, s1, f2, s2, s4, t1, t2, p1, p2,
+    f1, s1, f2, s2, t1, t2, p1, p2,
     local_sem, send_sem, recv_sem,
 ):
     mem, lat = lax.axis_index("mem"), lax.axis_index("lat")
@@ -138,12 +135,11 @@
         return {"mem": there, "lat": lat}
 
     z_up, z_down = member(0, 1, 0), member(0, NZ - 1, 0)
-    y_up, y_down = member(0, 0, 1), member(0, 0, NY - 1)
-    x_far, x_up, x_down = member(1, 0, 0), member(1, 1, 0), member(1, NZ - 1, 0)
     chip_lat = lax.rem(lat + 2, 4)
     chip = {"mem": mem, "lat": chip_lat}
     core = {"mem": mem, "lat": lat + 1 - 2 * lax.rem(lat, 2)}
-    plane = [(dx, dy) for dx in range(2) for dy in range(NY) if (dx, dy) != (0, 0)]
+    plane = [(1, 2), (0, 2), (1, 1), (1, 3), (0, 1), (0, 3), (1, 0)]
+    turns = (4, 3, 5, 2, 6, 1, 7)
     copies = Copies(send_sem, recv_sem)
 
     loads = [
@@ -156,13 +152,13 @@
 
     barrier = pltpu.get_barrier_semaphore()
     peers = [member(dx, 0, dy) for dx, dy in plane]
-    peers += [z_up, z_down, x_up, x_down, chip, core]
+    peers += [member(0, dz, 0) for dz in turns] + [chip, core]
     for peer in peers:
         pl.semaphore_signal(barrier, inc=1, device_id=peer, device_id_type=MESH)
     yu[xh, y] = jnp.zeros((ONE, 128), BF16)
     yu[xh, y, :, 0:UNIT] = grad[0:ONE]
-    zu[z, xh] = jnp.zeros((TWO, 128), BF16)
-    zu[z, xh, 0:REAL, 0:UNIT] = grad[ONE:ROWS]
+    zu[z] = jnp.zeros((TWO, 128), BF16)
+    zu[z, 0:REAL, 0:UNIT] = grad[ONE:ROWS]
     pl.semaphore_wait(barrier, len(peers))
 
     pieces = []
@@ -249,7 +245,12 @@
         for i in range(2):
             for j in range(NY):
                 gz[z, i, :, UNIT * j : UNIT * (j + 1)] = yu[i, j, :, 0:UNIT]
-        for t in gather_ring(copies, NZ, z, gz, 1, z_up, z_down):
+        cuts = (pl.ds(0, CUT), pl.ds(CUT, ONE - CUT))
+
+        def pick(d, part):
+            return gz.at[d, part // 2, cuts[part % 2]]
+
+        for t in gather_ring(copies, NZ, z, pick, 4, z_up, z_down):
             if t == 3:
                 piece_one(lax.rem(z + 2, 4))
             if t == 4:
@@ -259,41 +260,30 @@
         piece_one(lax.rem(z, 4))
 
     def color_two():
-        mine = zu.at[z, xh]
-        up = [copies.start(mine, mine, z_up)]
-        down = [copies.start(mine, mine, z_down)]
-        far = copies.start(mine, mine, x_far)
-        up.append(copies.start(mine, mine, x_up))
-        down.append(copies.start(mine, mine, x_down))
-        for t in range(1, NZ // 2):
-            yield
-            for copy in up:
-                copy.wait_recv()
-            there = zu.at[lax.rem(z + NZ - t, NZ)]
-            if t == NZ // 2 - 1:
-                there = zu.at[lax.rem(z + NZ - t, NZ), pl.ds(0, 1)]
-            up = [copies.start(there, there, z_up)]
-            for copy in down:
-                copy.wait_recv()
-            there = zu.at[lax.rem(z + t, NZ)]
-            if t == NZ // 2 - 1:
-                there = zu.at[lax.rem(z + t, NZ), pl.ds(1, 1)]
-            down = [copies.start(there, there, z_down)]
-        yield
-        for copy in (far, *up, *down):
+        mine = zu.at[z]
+        arriving = [copies.start(mine, mine, member(0, dz, 0)) for dz in turns]
+        yield
+        for copy in arriving:
             copy.wait_recv()
         for i in range(2):
-            for j in range(NZ):
-                v, r = 2 * i + j // 4, j % 4
-                gy[y, v, :, UNIT * r : UNIT * (r + 1)] = zu[j, i, :, 0:UNIT]
-        for t in gather_ring(copies, NY, y, gy, 2, y_up, y_down):
-            if t == 1:
-                piece_two(y)
-            if t == 2:
-                piece_two(lax.rem(y + 1, NY))
-                piece_two(lax.rem(y + 3, NY))
+            for r in range(4):
+                gy[y, 2 * xh + i, :, UNIT * r : UNIT * (r + 1)] = zu[4 * i + r, :, 0:UNIT]
+        mine = gy.at[y, pl.ds(2 * xh, 2)]
+        across = copies.start(mine, mine, member(1, 0, 0))
+        arriving = {
+            dy: [copies.start(mine, mine, member(0, 0, dy))] for dy in (1, 3, 2)
+        }
+        yield
+        across.wait_recv()
+        other = gy.at[y, pl.ds(2 - 2 * xh, 2)]
+        for dy in (1, 3, 2):
+            arriving[dy].append(copies.start(other, other, member(0, 0, dy)))
+        piece_two(y)
+        for dy in (1, 3, 2):
             yield
-        piece_two(lax.rem(y + 2, NY))
+            for copy in arriving[dy]:
+                copy.wait_recv()
+            piece_two(lax.rem(y + NY - dy, NY))
 
     def stage_zeros():
         for q in range(2 * NZ):
@@ -306,8 +296,8 @@
                 py[i, v, REAL:, :] = jnp.zeros((TWO - REAL, LANES), BF16)
         for i in range(2):
             gz[z, i, :, WIDE:] = jnp.zeros((ONE, LANES - WIDE), BF16)
-        for v in range(4):
-            gy[y, v, :, WIDE:] = jnp.zeros((TWO, LANES - WIDE), BF16)
+        for v in range(2):
+            gy[y, 2 * xh + v, :, WIDE:] = jnp.zeros((TWO, LANES - WIDE), BF16)
 
     def stage_pz(v):
         for r in range(4):
@@ -375,39 +365,38 @@
     next(two)
     stage_zeros()
     loads[0].wait()
+    next(one)
     stage_pz(0)
-    next(one)
     stage_pz(1)
     next(two)
     stage_pz(2)
     stage_pz(3)
     next(one)
-    next(two)
-    stage_py(0)
-    stage_py(1)
+    for k in range(4):
+        stage_py(k)
     next(two)
     next(one)
-    stage_py(2)
-    stage_py(3)
     next(two)
+    next(two)
+    pass_piece(0)
     next(one)
+    next(two, None)
+    pass_piece(1)
     stage_mix()
+    pass_piece(2)
+    next(one, None)
     stage_lags()
-    pass_piece(0)
-    next(one, None)
-    stage_kernel(0)
-    pass_piece(1)
-    stage_kernel(1)
-    pass_piece(2)
-    next(two)
-    stage_kernel(2)
-    stage_kernel(3)
-    next(two, None)
+    for k in range(4):
+        stage_kernel(k)
     pass_piece(3)
-    for k in range(4):
-        mix_piece(k)
-        pass_piece(4 + k)
+    mix_piece(0)
+    mix_piece(1)
+    pass_piece(4)
+    mix_piece(2)
+    mix_piece(3)
     for k in range(4, 8):
+        if k + 1 < 8:
+            pass_piece(k + 1)
         mix_piece(k)
 
     def restore(rows):
@@ -431,10 +420,6 @@
         for i in range(NY):
             t1[j, i, :, 0:UNIT] = value[:, UNIT * i : UNIT * (i + 1)]
 
-    def store_two(j, value):
-        for r in range(4):
-            t2[r + 4 * (j % 2), j // 2, :, 0:UNIT] = value[:, UNIT * r : UNIT * (r + 1)]
-
     scale = 1.0 / math.sqrt(MEMBERS - 1)
 
     def sum_one():
@@ -460,49 +445,34 @@
                 rest_y[i, :, UNIT * r : UNIT * (r + 1)] = rest[
                     r, ONE : ONE + FLOAT, UNIT * i : UNIT * (i + 1)
                 ]
-        yield from scatter_ring(
-            copies, NY, y, term_two, f2, s2, 2, y_up, y_down, store_two
-        )
-        last = NZ // 2 - 1
-        far = lax.rem(z + NZ // 2, NZ)
-        cross = copies.start(t2.at[z, 1 - xh], p2.at[4], x_far)
-        up = copies.start(t2.at[far, pl.ds(0, 1)], s4.at[0, 0, pl.ds(0, 1)], z_up)
-        down = copies.start(t2.at[far, pl.ds(1, 1)], s4.at[1, 0, pl.ds(1, 1)], z_down)
-        for t in range(1, NZ // 2):
-            yield
-            made = []
-            for way, copy, dest, near, aside in (
-                (0, up, lax.rem(z + NZ // 2 - t, NZ), z_up, x_up),
-                (1, down, lax.rem(z + NZ // 2 + t, NZ), z_down, x_down),
-            ):
-                copy.wait_recv()
-                for j in range(2):
-                    if t == 1 and j != way:
-                        s4[way, t - 1, j] = t2[dest, j]
-                    else:
-                        s4[way, t - 1, j] += t2[dest, j]
-                if t < last:
-                    made.append(copies.start(s4.at[way, t - 1], s4.at[way, t], near))
-                else:
-                    made.append(
-                        (
-                            copies.start(s4.at[way, t - 1, xh], p2.at[2 * way], near),
-                            copies.start(
-                                s4.at[way, t - 1, 1 - xh], p2.at[2 * way + 1], aside
-                            ),
-                        )
-                    )
-            up, down = made
-        yield
-        for copy in (cross, *up, *down):
+        arriving = []
+        for k, (dx, dy) in enumerate(plane):
+            to_x, to_y = lax.rem(xh + dx, 2), lax.rem(y + dy, NY)
+            for i in range(2):
+                f2[k, i] = term_two(to_y, 2 * to_x + i)
+            arriving.append(copies.start(f2.at[k], s2.at[k], member(dx, 0, dy)))
+        yield
+        for i in range(2):
+            total = term_two(y, 2 * xh + i)
+            for k, copy in enumerate(arriving):
+                if i == 0:
+                    copy.wait_recv()
+                total += s2[k, i]
+            for r in range(4):
+                t2[4 * i + r, :, 0:UNIT] = total[:, UNIT * r : UNIT * (r + 1)]
+        arriving = []
+        for k, dz in enumerate(turns):
+            part = t2.at[lax.rem(z + dz, NZ)]
+            arriving.append(copies.start(part, p2.at[k], member(0, dz, 0)))
+        yield
+        total = t2[z]
+        for k, copy in enumerate(arriving):
             copy.wait_recv()
-        total = t2[z, xh]
-        for k in range(5):
             total += p2[k]
         out[ONE:ROWS, :] = (total * scale)[0:REAL, 0:UNIT]
 
     one, two = sum_one(), sum_two()
-    for chain in (one, two, one, two, one, two, one, two, two, one, two, two, one):
+    for chain in (one, two, one, one, one, two, one, two, one):
         next(chain, None)
     for copy in copies.made:
         copy.wait_send()
@@ -521,7 +491,7 @@
             pltpu.VMEM((720, 720), F32),
             pltpu.VMEM((NWAVE, TABLE), F32),
             pltpu.VMEM((2, NY, ONE, 128), BF16),
-            pltpu.VMEM((NZ, 2, TWO, 128), BF16),
+            pltpu.VMEM((NZ, TWO, 128), BF16),
             pltpu.VMEM((NZ, 2, ONE, LANES), BF16),
             pltpu.VMEM((NY, 4, TWO, LANES), BF16),
             pltpu.VMEM((2 * NZ, ONE, LANES), BF16),
@@ -542,13 +512,12 @@
             pltpu.VMEM((NY, FLOAT, LANES), F32),
             pltpu.VMEM((2, 2, ONE, LANES), F32),
             pltpu.VMEM((2, NZ // 2, 2, ONE, LANES), F32),
-            pltpu.VMEM((2, 4, FLOAT, LANES), F32),
-            pltpu.VMEM((2, NY // 2, 4, FLOAT, LANES), F32),
-            pltpu.VMEM((2, NZ // 2 - 1, 2, FLOAT, 128), F32),
+            pltpu.VMEM((7, 2, FLOAT, LANES), F32),
+            pltpu.VMEM((7, 2, FLOAT, LANES), F32),
             pltpu.VMEM((2, NY, ONE, 128), F32),
-            pltpu.VMEM((NZ, 2, FLOAT, 128), F32),
+            pltpu.VMEM((NZ, FLOAT, 128), F32),
             pltpu.VMEM((7, ONE, 128), F32),
-            pltpu.VMEM((5, FLOAT, 128), F32),
+            pltpu.VMEM((7, FLOAT, 128), F32),
             pltpu.SemaphoreType.DMA((3,)),
             pltpu.SemaphoreType.DMA((128,)),
             pltpu.SemaphoreType.DMA((128,)),

time: 102 us -> 94.8 us (0.929)
  Pallas kernels: 100 us -> 92.1 us
    pallas_call x1, Pallas kernels: 100 us -> 92.1 us  [local(): pl.pallas_call(kernel, out_shape=jax.ShapeDtypeStruct((ROWS, UNIT), F32),...]
where the time goes in v2:
time: 94.8 us; the launch traced here: 93.7 us
  Pallas kernels  92.1 us (97%)
  local copies, waits for them, and re-layouts  1.54 us (2%)
    pallas_call x1, Pallas kernels, local(): pl.pallas_call(kernel, out_shape=jax.ShapeDtypeStruct((ROWS, UNIT), F32),...  92.1 us

profile of v2, /device:TPU:8, one launch (start us, length us, event | category | flops | bytes accessed | tf_op | source)
XLA Modules:
  0.0 93.7 jit_solution(14602837552348124304)
XLA Ops:
  0.0 92.1 %shard_map.55 = f32[180,90]{1,0:T(8,128)} custom-call(bf16[180,5760]{1,0:T(8,128)(2,1)} %bitcast.1, bf16[180,90]{1,0:T(8,128)(2,1)} %grad.1, f32[720,720]{1,0:T(8,128)} %mix.1, f32[720]{0:T(1024)} %weight.1, f32[720,1920]{1,0:T(8,128)} %constant.2.clone.table), custom_call_target="tpu_custom_call" | custom-call | tf_op jit(solution)/shard_map/pallas_call | solution.py:484
  92.1 1.5 %copy.7 = f32[180,90]{1,0:T(8,128)} copy(f32[180,90]{1,0:T(8,128)} %shard_map.55) | data formatting | bytes 129600

commit v3 on v2

--- a/solution.py
+++ b/solution.py
@@ -24,6 +24,7 @@
 UNIT = 90
 WIDE = 360
 LANES = 384
+FREE = WIDE - 256
 NZ, NY = 8, 4
 LEFT = 384
 TABLE = 1920
@@ -55,6 +56,28 @@
         copy.start()
         self.made.append(copy)
         return copy
+
+
+def packed(value):
+    lane = lax.broadcasted_iota(jnp.int32, (value.shape[0], 128), 1)
+    most = jnp.max(jnp.abs(value), axis=1, keepdims=True)
+    level = jnp.ceil(jnp.log(jnp.maximum(most, 1e-30) / 32000.0) * (8.0 / math.log(2.0)))
+    whole = jnp.floor(value * jnp.exp(level * (-math.log(2.0) / 8.0)) + 0.5)
+    a, b, c = whole[:, 0:128], whole[:, 128:256], whole[:, 256:384]
+    c = jnp.where(lane < FREE, c, level)
+    high = jnp.floor(b * (1.0 / 256.0) + 0.5)
+    return jnp.concatenate([a * 256.0 + high, c * 256.0 + (b - high * 256.0)], axis=1)
+
+
+def unpacked(words):
+    lane = lax.broadcasted_iota(jnp.int32, (words.shape[0], 128), 1)
+    first, second = words[:, 0:128], words[:, 128:256]
+    a = jnp.floor(first * (1.0 / 256.0) + 0.5)
+    c = jnp.floor(second * (1.0 / 256.0) + 0.5)
+    b = (first - a * 256.0) * 256.0 + (second - c * 256.0)
+    scale = jnp.exp(c[:, FREE : FREE + 1] * (math.log(2.0) / 8.0))
+    c = jnp.where(lane < FREE, c, 0.0)
+    return jnp.concatenate([a * scale, b * scale, c * scale], axis=1)
 
 
 def gather_ring(copies, n, me, pick, parts, plus, minus):
@@ -120,7 +143,7 @@
 
 def kernel(
     pert, grad, mix, weight, table, out,
-    p_v, m_v, e_v, yu, zu, gz, gy, pz, py, work, own_two, ag_one, ag_two,
+    p_v, m_v, e_v, yu, zu, gz, gy, pz, py, work, own_two, ag_one, ag_two, pk_one, pk_two,
     mpad, mh_one, ml_one, mh_two, ml_two, ch, cl, local, rest, rest_y,
     f1, s1, f2, s2, t1, t2, p1, p2,
     local_sem, send_sem, recv_sem,
@@ -166,26 +189,44 @@
     def band_rows(b, rows):
         return pl.ds(pl.multiple_of(b * rows, 16), rows)
 
-    def send_piece(ag, index, rows, value):
+    def send_piece(first, index, value):
+        ag, pack = (ag_one, pk_one) if first else (ag_two, pk_two)
+        rows, sent = value.shape[0], pack.shape[2]
+        pack[index, lat] = packed(value[0:sent])
+        here = pack.at[index, lat]
+        over = copies.start(here, here, chip)
         high = value.astype(BF16)
         ag[index, band_rows(lat, rows), 0:LANES] = high
         ag[index, band_rows(lat, rows), LANES:] = (value - high.astype(F32)).astype(BF16)
         here = ag.at[index, band_rows(lat, rows)]
-        there = ag.at[index, band_rows(chip_lat, rows)]
         pieces.append(
             {
                 "index": index,
-                "one": rows == ONE,
-                "there": there,
-                "chip": copies.start(here, here, chip),
+                "one": first,
+                "ag": ag,
+                "pack": pack,
+                "rows": rows,
+                "chip": over,
                 "core": copies.start(here, here, core),
             }
         )
+
+    def unpack_piece(piece, b):
+        value = unpacked(piece["pack"][piece["index"], b])
+        rows, sent = piece["rows"], value.shape[0]
+        if sent < rows:
+            value = jnp.concatenate([value, jnp.zeros((rows - sent, LANES), F32)], axis=0)
+        high = value.astype(BF16)
+        low = (value - high.astype(F32)).astype(BF16)
+        piece["ag"][piece["index"], band_rows(b, rows), 0:LANES] = high
+        piece["ag"][piece["index"], band_rows(b, rows), LANES:] = low
 
     def pass_piece(k):
         piece = pieces[k]
         piece["chip"].wait_recv()
-        piece["passed"] = copies.start(piece["there"], piece["there"], core)
+        there = piece["pack"].at[piece["index"], chip_lat]
+        piece["passed"] = copies.start(there, there, core)
+        unpack_piece(piece, chip_lat)
 
     def mixed(high, low, ag, index):
         both = jnp.dot(high[...], ag[index], preferred_element_type=F32)
@@ -198,6 +239,7 @@
         piece = pieces[k]
         piece["core"].wait_recv()
         piece["passed"].wait_recv()
+        unpack_piece(piece, chip_lat + 1 - 2 * lax.rem(lat, 2))
         index = piece["index"]
         if piece["one"]:
             local[index] += mixed(mh_one, ml_one, ag_one, index)
@@ -218,14 +260,14 @@
         total = jnp.zeros((ONE, LANES), F32)
         for v in range(4):
             total += pz[4 * v + r].astype(F32) * gz[r + 4 * (v % 2), v // 2].astype(F32)
-        send_piece(ag_one, r, ONE, total)
+        send_piece(True, r, total)
         local[r, 0:ONE] += total
 
     def piece_two(i):
         total = jnp.zeros((TWO, LANES), F32)
         for v in range(4):
             total += py[i, v].astype(F32) * gy[i, v].astype(F32)
-        send_piece(ag_two, i, TWO, total)
+        send_piece(False, i, total)
         own_two[0:TWO] = total
         for i_ in range(NY):
 
@@ -500,6 +542,8 @@
             pltpu.VMEM((BAND, LANES), F32),
             pltpu.VMEM((4, 4 * ONE, 2 * LANES), BF16),
             pltpu.VMEM((4, 4 * TWO, 2 * LANES), BF16),
+            pltpu.VMEM((4, 4, ONE, 256), F32),
+            pltpu.VMEM((4, 4, FLOAT, 256), F32),
             pltpu.VMEM((BAND, 4 * BAND), F32),
             pltpu.VMEM((BAND, 4 * ONE), BF16),
             pltpu.VMEM((BAND, 4 * ONE), BF16),

time: 94.8 us -> 88.8 us (0.937)
  Pallas kernels: 92.1 us -> 86.7 us
    pallas_call x1, Pallas kernels: 92.1 us -> 86.7 us  [local(): pl.pallas_call(kernel, out_shape=jax.ShapeDtypeStruct((ROWS, UNIT), F32),...]
where the time goes in v3:
time: 88.8 us; the launch traced here: 88.3 us
  Pallas kernels  86.7 us (98%)
  local copies, waits for them, and re-layouts  1.54 us (2%)
    pallas_call x1, Pallas kernels, local(): pl.pallas_call(kernel, out_shape=jax.ShapeDtypeStruct((ROWS, UNIT), F32),...  86.7 us

profile of v3, /device:TPU:8, one launch (start us, length us, event | category | flops | bytes accessed | tf_op | source)
XLA Modules:
  0.0 88.3 jit_solution(17103541370831148131)
XLA Ops:
  0.0 86.7 %shard_map.55 = f32[180,90]{1,0:T(8,128)} custom-call(bf16[180,5760]{1,0:T(8,128)(2,1)} %bitcast.1, bf16[180,90]{1,0:T(8,128)(2,1)} %grad.1, f32[720,720]{1,0:T(8,128)} %mix.1, f32[720]{0:T(1024)} %weight.1, f32[720,1920]{1,0:T(8,128)} %constant.2.clone.table), custom_call_target="tpu_custom_call" | custom-call | tf_op jit(solution)/shard_map/pallas_call | solution.py:526
  86.7 1.5 %copy.7 = f32[180,90]{1,0:T(8,128)} copy(f32[180,90]{1,0:T(8,128)} %shard_map.55) | data formatting | bytes 129600

commit v4 on v3

--- a/solution.py
+++ b/solution.py
@@ -144,8 +144,8 @@
 def kernel(
     pert, grad, mix, weight, table, out,
     p_v, m_v, e_v, yu, zu, gz, gy, pz, py, work, own_two, ag_one, ag_two, pk_one, pk_two,
-    mpad, mh_one, ml_one, mh_two, ml_two, ch, cl, local, rest, rest_y,
-    f1, s1, f2, s2, t1, t2, p1, p2,
+    mpad, mh_one, ml_one, mh_two, ml_two, blocks, sum_h, sum_l, odd_h, odd_l, local, rest, rest_y,
+    f1, s1, t1, p1, f3, s3, t3, p3, f2, s2, t2, p2,
     local_sem, send_sem, recv_sem,
 ):
     mem, lat = lax.axis_index("mem"), lax.axis_index("lat")
@@ -379,28 +379,34 @@
             row, e_v[...], precision=lax.Precision.HIGHEST, preferred_element_type=F32
         )
 
-    def stage_kernel(d):
-        lags = jnp.concatenate(
-            [
-                work[0:1, LEFT + WIDE * d : LEFT + WIDE * d + LANES],
-                work[0:1, WIDE * d : WIDE * d + LEFT],
-            ],
-            axis=1,
-        )
-        turned = pltpu.roll(
-            jnp.broadcast_to(lags, (LANES, 2 * LANES)), 0, 1, stride=1, stride_axis=0
-        )
-        block = turned[:, :LANES]
-        high = block.astype(BF16)
-        low = (block - high.astype(F32)).astype(BF16)
-        for r in range(4):
-            s = (r + d) % 4
-            place = (
-                slice(LANES * r, LANES * (r + 1)),
-                slice(LANES * s, LANES * (s + 1)),
+    def stage_kernel():
+        for d in range(4):
+            lags = jnp.concatenate(
+                [
+                    work[0:1, LEFT + WIDE * d : LEFT + WIDE * d + LANES],
+                    work[0:1, WIDE * d : WIDE * d + LEFT],
+                ],
+                axis=1,
             )
-            ch[place] = high
-            cl[place] = low
+            turned = pltpu.roll(
+                jnp.broadcast_to(lags, (LANES, 2 * LANES)), 0, 1, stride=1, stride_axis=0
+            )
+            blocks[d] = turned[:, :LANES]
+
+        def keep(high_ref, low_ref, place, block):
+            high = block.astype(BF16)
+            high_ref[place] = high
+            low_ref[place] = (block - high.astype(F32)).astype(BF16)
+
+        left, right = slice(0, LANES), slice(LANES, 2 * LANES)
+        first, second = blocks[0] + blocks[2], blocks[1] + blocks[3]
+        keep(sum_h, sum_l, (0,), (first + second) * 0.25)
+        keep(sum_h, sum_l, (1,), (first - second) * 0.25)
+        first, second = (blocks[0] - blocks[2]) * 0.5, (blocks[1] - blocks[3]) * 0.5
+        keep(odd_h, odd_l, (left, left), first)
+        keep(odd_h, odd_l, (right, right), first)
+        keep(odd_h, odd_l, (left, right), second)
+        keep(odd_h, odd_l, (right, left), -second)
 
     one, two = color_one(), color_two()
     next(one)
@@ -425,11 +431,10 @@
     next(two, None)
     pass_piece(1)
     stage_mix()
+    stage_lags()
+    stage_kernel()
     pass_piece(2)
     next(one, None)
-    stage_lags()
-    for k in range(4):
-        stage_kernel(k)
     pass_piece(3)
     mix_piece(0)
     mix_piece(1)
@@ -441,34 +446,44 @@
             pass_piece(k + 1)
         mix_piece(k)
 
-    def restore(rows):
-        value = jnp.concatenate([local[r, rows] for r in range(4)], axis=1)
+    def product(value, high_ref, low_ref):
         high = value.astype(BF16)
         low = (value - high.astype(F32)).astype(BF16)
-        for s in range(4):
-            cols = slice(LANES * s, LANES * (s + 1))
-            rest[s, rows] = jnp.dot(high, ch[:, cols], preferred_element_type=F32) + (
-                jnp.dot(high, cl[:, cols], preferred_element_type=F32)
-                + jnp.dot(low, ch[:, cols], preferred_element_type=F32)
-            )
-
-    def term_one(d, j):
-        return pz[j * NZ + d].astype(F32) * rest[lax.rem(d, 4), 0:ONE]
+        return jnp.dot(high, high_ref, preferred_element_type=F32) + (
+            jnp.dot(high, low_ref, preferred_element_type=F32)
+            + jnp.dot(low, high_ref, preferred_element_type=F32)
+        )
+
+    even_0, even_1 = local[0] + local[2], local[1] + local[3]
+    odd = jnp.concatenate([local[0] - local[2], local[1] - local[3]], axis=1)
+    even_0, even_1 = (
+        product(even_0 + even_1, sum_h[0], sum_l[0]),
+        product(even_0 - even_1, sum_h[1], sum_l[1]),
+    )
+    even_0, even_1 = even_0 + even_1, even_0 - even_1
+    odd_0 = product(odd, odd_h[:, 0:LANES], odd_l[:, 0:LANES])
+    odd_1 = product(odd, odd_h[:, LANES:], odd_l[:, LANES:])
+    rest[0] = even_0 + odd_0
+    rest[1] = even_1 + odd_1
+    rest[2] = even_0 - odd_0
+    rest[3] = even_1 - odd_1
 
     def term_two(d, j):
         return py[d, j, 0:FLOAT].astype(F32) * rest_y[d]
 
-    def store_one(j, value):
-        for i in range(NY):
-            t1[j, i, :, 0:UNIT] = value[:, UNIT * i : UNIT * (i + 1)]
-
     scale = 1.0 / math.sqrt(MEMBERS - 1)
 
-    def sum_one():
-        restore(slice(0, ONE))
-        yield from scatter_ring(
-            copies, NZ, z, term_one, f1, s1, 1, z_up, z_down, store_one
-        )
+    def sum_one(first, last, f1, s1, t1, p1):
+        rows = slice(first, last)
+
+        def term(d, j):
+            return pz[j * NZ + d, rows].astype(F32) * rest[lax.rem(d, 4), rows]
+
+        def store(j, value):
+            for i in range(NY):
+                t1[j, i, :, 0:UNIT] = value[:, UNIT * i : UNIT * (i + 1)]
+
+        yield from scatter_ring(copies, NZ, z, term, f1, s1, 1, z_up, z_down, store)
         arriving = []
         for k, (dx, dy) in enumerate(plane):
             part = t1.at[lax.rem(xh + dx, 2), lax.rem(y + dy, NY)]
@@ -478,10 +493,9 @@
         for k, copy in enumerate(arriving):
             copy.wait_recv()
             total += p1[k]
-        out[0:ONE, :] = (total * scale)[:, 0:UNIT]
+        out[rows, :] = (total * scale)[:, 0:UNIT]
 
     def sum_two():
-        restore(slice(ONE, BAND))
         for i in range(NY):
             for r in range(4):
                 rest_y[i, :, UNIT * r : UNIT * (r + 1)] = rest[
@@ -513,8 +527,10 @@
             total += p2[k]
         out[ONE:ROWS, :] = (total * scale)[0:REAL, 0:UNIT]
 
-    one, two = sum_one(), sum_two()
-    for chain in (one, two, one, one, one, two, one, two, one):
+    one = sum_one(0, CUT, f1, s1, t1, p1)
+    also = sum_one(CUT, ONE, f3, s3, t3, p3)
+    two = sum_two()
+    for chain in (one, also, two, one, also, one, also, one, also, two, one, also, two, one, also):
         next(chain, None)
     for copy in copies.made:
         copy.wait_send()
@@ -549,22 +565,29 @@
             pltpu.VMEM((BAND, 4 * ONE), BF16),
             pltpu.VMEM((BAND, 4 * TWO), BF16),
             pltpu.VMEM((BAND, 4 * TWO), BF16),
-            pltpu.VMEM((4 * LANES, 4 * LANES), BF16),
-            pltpu.VMEM((4 * LANES, 4 * LANES), BF16),
+            pltpu.VMEM((4, LANES, LANES), F32),
+            pltpu.VMEM((2, LANES, LANES), BF16),
+            pltpu.VMEM((2, LANES, LANES), BF16),
+            pltpu.VMEM((2 * LANES, 2 * LANES), BF16),
+            pltpu.VMEM((2 * LANES, 2 * LANES), BF16),
             pltpu.VMEM((4, BAND, LANES), F32),
             pltpu.VMEM((4, BAND, LANES), F32),
             pltpu.VMEM((NY, FLOAT, LANES), F32),
-            pltpu.VMEM((2, 2, ONE, LANES), F32),
-            pltpu.VMEM((2, NZ // 2, 2, ONE, LANES), F32),
+            pltpu.VMEM((2, 2, CUT, LANES), F32),
+            pltpu.VMEM((2, NZ // 2, 2, CUT, LANES), F32),
+            pltpu.VMEM((2, NY, CUT, 128), F32),
+            pltpu.VMEM((7, CUT, 128), F32),
+            pltpu.VMEM((2, 2, ONE - CUT, LANES), F32),
+            pltpu.VMEM((2, NZ // 2, 2, ONE - CUT, LANES), F32),
+            pltpu.VMEM((2, NY, ONE - CUT, 128), F32),
+            pltpu.VMEM((7, ONE - CUT, 128), F32),
             pltpu.VMEM((7, 2, FLOAT, LANES), F32),
             pltpu.VMEM((7, 2, FLOAT, LANES), F32),
-            pltpu.VMEM((2, NY, ONE, 128), F32),
             pltpu.VMEM((NZ, FLOAT, 128), F32),
-            pltpu.VMEM((7, ONE, 128), F32),
             pltpu.VMEM((7, FLOAT, 128), F32),
             pltpu.SemaphoreType.DMA((3,)),
-            pltpu.SemaphoreType.DMA((128,)),
-            pltpu.SemaphoreType.DMA((128,)),
+            pltpu.SemaphoreType.DMA((160,)),
+            pltpu.SemaphoreType.DMA((160,)),
         ],
         compiler_params=pltpu.CompilerParams(
             collective_id=0, has_side_effects=True, vmem_limit_bytes=56 * 2**20

time: 88.8 us -> 85.7 us (0.965)
  Pallas kernels: 86.7 us -> 84 us
    pallas_call x1, Pallas kernels: 86.7 us -> 84 us  [local(): pl.pallas_call(kernel, out_shape=jax.ShapeDtypeStruct((ROWS, UNIT), F32),...]
where the time goes in v4:
time: 85.7 us; the launch traced here: 85.5 us
  Pallas kernels  84 us (98%)
  local copies, waits for them, and re-layouts  1.54 us (2%)
    pallas_call x1, Pallas kernels, local(): pl.pallas_call(kernel, out_shape=jax.ShapeDtypeStruct((ROWS, UNIT), F32),...  84 us

profile of v4, /device:TPU:8, one launch (start us, length us, event | category | flops | bytes accessed | tf_op | source)
XLA Modules:
  0.0 85.5 jit_solution(9091376511342336742)
XLA Ops:
  0.0 84.0 %shard_map.55 = f32[180,90]{1,0:T(8,128)} custom-call(bf16[180,5760]{1,0:T(8,128)(2,1)} %bitcast.1, bf16[180,90]{1,0:T(8,128)(2,1)} %grad.1, f32[720,720]{1,0:T(8,128)} %mix.1, f32[720]{0:T(1024)} %weight.1, f32[720,1920]{1,0:T(8,128)} %constant.2.clone.table), custom_call_target="tpu_custom_call" | custom-call | tf_op jit(solution)/shard_map/pallas_call | solution.py:542
  84.0 1.5 %copy.7 = f32[180,90]{1,0:T(8,128)} copy(f32[180,90]{1,0:T(8,128)} %shard_map.55) | data formatting | bytes 129600

commit v5 on v4

--- a/solution.py
+++ b/solution.py
@@ -439,12 +439,15 @@
     mix_piece(0)
     mix_piece(1)
     pass_piece(4)
+    pass_piece(5)
     mix_piece(2)
     mix_piece(3)
-    for k in range(4, 8):
-        if k + 1 < 8:
-            pass_piece(k + 1)
-        mix_piece(k)
+    pass_piece(6)
+    mix_piece(4)
+    mix_piece(5)
+    pass_piece(7)
+    mix_piece(6)
+    mix_piece(7)
 
     def product(value, high_ref, low_ref):
         high = value.astype(BF16)

time: 85.7 us -> 86.1 us (level); the launches traced: 85.5 us -> 84.6 us
  Pallas kernels: 84 us -> 83.1 us
    pallas_call x1, Pallas kernels: 84 us -> 83.1 us  [local(): pl.pallas_call(kernel, out_shape=jax.ShapeDtypeStruct((ROWS, UNIT), F32),...]
where the time goes in v5:
time: 86.1 us; the launch traced here: 84.6 us
  Pallas kernels  83.1 us (97%)
  local copies, waits for them, and re-layouts  1.54 us (2%)
    pallas_call x1, Pallas kernels, local(): pl.pallas_call(kernel, out_shape=jax.ShapeDtypeStruct((ROWS, UNIT), F32),...  83.1 us

profile of v5, /device:TPU:8, one launch (start us, length us, event | category | flops | bytes accessed | tf_op | source)
XLA Modules:
  0.0 84.6 jit_solution(10501318332201423140)
XLA Ops:
  0.0 83.1 %shard_map.55 = f32[180,90]{1,0:T(8,128)} custom-call(bf16[180,5760]{1,0:T(8,128)(2,1)} %bitcast.1, bf16[180,90]{1,0:T(8,128)(2,1)} %grad.1, f32[720,720]{1,0:T(8,128)} %mix.1, f32[720]{0:T(1024)} %weight.1, f32[720,1920]{1,0:T(8,128)} %constant.2.clone.table), custom_call_target="tpu_custom_call" | custom-call | tf_op jit(solution)/shard_map/pallas_call | solution.py:545
  83.1 1.5 %copy.7 = f32[180,90]{1,0:T(8,128)} copy(f32[180,90]{1,0:T(8,128)} %shard_map.55) | data formatting | bytes 129600

commit v6 on v4

--- a/solution.py
+++ b/solution.py
@@ -429,10 +429,10 @@
     pass_piece(0)
     next(one)
     next(two, None)
+    stage_lags()
+    stage_kernel()
     pass_piece(1)
     stage_mix()
-    stage_lags()
-    stage_kernel()
     pass_piece(2)
     next(one, None)
     pass_piece(3)

time: 85.7 us -> 85.2 us (level)
  Pallas kernels: 84 us -> 83.1 us
    pallas_call x1, Pallas kernels: 84 us -> 83.1 us  [local(): pl.pallas_call(kernel, out_shape=jax.ShapeDtypeStruct((ROWS, UNIT), F32),...]
where the time goes in v6:
time: 85.2 us; the launch traced here: 84.6 us
  Pallas kernels  83.1 us (98%)
  local copies, waits for them, and re-layouts  1.54 us (2%)
    pallas_call x1, Pallas kernels, local(): pl.pallas_call(kernel, out_shape=jax.ShapeDtypeStruct((ROWS, UNIT), F32),...  83.1 us

profile of v6, /device:TPU:8, one launch (start us, length us, event | category | flops | bytes accessed | tf_op | source)
XLA Modules:
  0.0 84.6 jit_solution(6989363333395947940)
XLA Ops:
  0.0 83.1 %shard_map.55 = f32[180,90]{1,0:T(8,128)} custom-call(bf16[180,5760]{1,0:T(8,128)(2,1)} %bitcast.1, bf16[180,90]{1,0:T(8,128)(2,1)} %grad.1, f32[720,720]{1,0:T(8,128)} %mix.1, f32[720]{0:T(1024)} %weight.1, f32[720,1920]{1,0:T(8,128)} %constant.2.clone.table), custom_call_target="tpu_custom_call" | custom-call | tf_op jit(solution)/shard_map/pallas_call | solution.py:542
  83.1 1.5 %copy.7 = f32[180,90]{1,0:T(8,128)} copy(f32[180,90]{1,0:T(8,128)} %shard_map.55) | data formatting | bytes 129600
